TPU v7x, 32 devices: a whole 2x2x4 slice. The times are simulated.
32 devices in a mesh: dp: 16 (over z, x, core), blk: 2 (over y).
Axes of the slice: x: 2, y: 2, z: 4, core: 2. Of those that a mesh axis runs over, the one named last changes fastest.
Arguments:
- waveform: bfloat16 [512, 330], P(('dp', 'blk')), may hold values from -6 to 6
- length_bin: int32 [512], P(('dp', 'blk')), may hold values from 1 to 4
- packing: int32 [32, 16], P(('dp', 'blk')), may hold values from 0 to 15, each once within a row
- cotangent: bfloat16 [512, 32, 512], P(('dp', 'blk')), may hold values from -6 to 6
- conv_one: bfloat16 [10, 512], replicated, may hold values from -2 to 2
- bias_one: float32 [512], replicated, may hold values from -6 to 6
- gain_one: float32 [512], replicated, may hold values from 2 to 8
- shift_one: float32 [512], replicated, may hold values from -12 to 12
- conv_two: bfloat16 [1536, 512], replicated, may hold values from -0.15625 to 0.15625
- bias_two: float32 [512], replicated, may hold values from -6 to 6
- gain_two: float32 [512], replicated, may hold values from 0.5 to 1.5
- shift_two: float32 [512], replicated, may hold values from -3 to 3
Outputs:
- grad_conv_two: float32 [1536, 512], P('dp')
- grad_small: float32 [16, 512], replicated
All inputs are finite; a program needn't handle non-finite values.
Results may differ from a plain program's by a relative error of at most 0.0046.
Values may be sent and summed in bfloat16 or wider, within the bound.
No kernel may reach another device: no remote copies, remote signals or barrier semaphores. Data moves between devices by JAX's collectives and lax.ppermute only.
A program may use at most 64 MiB of HBM per device.

v0:
```python
import jax
import jax.numpy as jnp
from jax import lax
from jax.sharding import PartitionSpec as P

NB = 4
GROUP = 8


def norm_act(z, gain, shift):
    mean = jnp.mean(z, axis=-1, keepdims=True)
    cent = z - mean
    var = jnp.mean(cent * cent, axis=-1, keepdims=True)
    rstd = lax.rsqrt(var + 1e-05)
    normed = cent * rstd
    return (normed * gain + shift, normed, rstd)


def gelu_exact(act):
    return 0.5 * act * (1.0 + lax.erf(act * 0.7071067811865476))


def norm_back(grad_out, act, normed, rstd, gain):
    cdf = 0.5 * (1.0 + lax.erf(act * 0.7071067811865476))
    pdf = jnp.exp(-0.5 * act * act) * 0.3989422804014327
    grad_act = grad_out * (cdf + act * pdf)
    grad_gain = jnp.sum(grad_act * normed, axis=0)
    grad_shift = jnp.sum(grad_act, axis=0)
    grad_norm = grad_act * gain
    inner = grad_norm - jnp.mean(grad_norm, axis=-1, keepdims=True)
    inner = inner - normed * jnp.mean(grad_norm * normed, axis=-1, keepdims=True)
    return (rstd * inner, grad_gain, grad_shift)


def pass_group(
    wave,
    bins,
    cot,
    conv_one,
    bias_one,
    gain_one,
    shift_one,
    conv_two,
    bias_two,
    gain_two,
    shift_two,
):
    count = wave.shape[0]
    frames_two = cot.shape[1]
    width = cot.shape[2]
    frames_one = 2 * frames_two + 1
    split = wave.reshape(count, frames_one + 1, 5)
    cols_one = jnp.concatenate([split[:, :-1], split[:, 1:]], axis=-1).reshape(
        count * frames_one, 10
    )
    z_one = jnp.dot(cols_one, conv_one, preferred_element_type=jnp.float32) + bias_one
    act_one, normed_one, rstd_one = norm_act(z_one, gain_one, shift_one)
    hidden = gelu_exact(act_one).astype(jnp.bfloat16).reshape(count, frames_one, width)
    cols_two = jnp.concatenate(
        [hidden[:, : 2 * frames_two].reshape(count, frames_two, 2 * width), hidden[:, 2::2]],
        axis=-1,
    )
    cols_two = cols_two.reshape(count * frames_two, 3 * width)
    z_two = jnp.dot(cols_two, conv_two, preferred_element_type=jnp.float32) + bias_two
    act_two, normed_two, rstd_two = norm_act(z_two, gain_two, shift_two)
    limit = bins * frames_two // NB
    valid = (jnp.arange(frames_two, dtype=jnp.int32)[None, :] < limit[:, None]).astype(jnp.float32)
    grad_out = (cot.astype(jnp.float32) * valid[:, :, None]).reshape(count * frames_two, width)
    dz_two, dgain_two, dshift_two = norm_back(grad_out, act_two, normed_two, rstd_two, gain_two)
    dbias_two = jnp.sum(dz_two, axis=0)
    dz_two_b = dz_two.astype(jnp.bfloat16)
    dcols = jnp.dot(dz_two_b, conv_two.T, preferred_element_type=jnp.float32).reshape(
        count, frames_two, 3 * width
    )
    part_a = dcols[:, :, : 2 * width].reshape(count, 2 * frames_two, width)
    part_b = dcols[:, :, 2 * width :]
    spread = jnp.stack([part_b, jnp.zeros_like(part_b)], axis=2).reshape(
        count, 2 * frames_two, width
    )
    zero_one = jnp.zeros((count, 1, width), jnp.float32)
    zero_two = jnp.zeros((count, 2, width), jnp.float32)
    dhidden = jnp.concatenate([part_a, zero_one], axis=1) + jnp.concatenate(
        [zero_two, spread[:, : 2 * frames_two - 1]], axis=1
    )
    dz_one, dgain_one, dshift_one = norm_back(
        dhidden.reshape(count * frames_one, width), act_one, normed_one, rstd_one, gain_one
    )
    dbias_one = jnp.sum(dz_one, axis=0)
    dconv_one = jnp.dot(cols_one.T, dz_one.astype(jnp.bfloat16), preferred_element_type=jnp.float32)
    small = jnp.concatenate(
        [
            dconv_one,
            jnp.stack([dbias_one, dgain_one, dshift_one, dbias_two, dgain_two, dshift_two]),
        ],
        axis=0,
    )
    return (cols_two, dz_two_b, small)


def per_device(
    waveform,
    length_bin,
    packing,
    cotangent,
    conv_one,
    bias_one,
    gain_one,
    shift_one,
    conv_two,
    bias_two,
    gain_two,
    shift_two,
):
    order_list = packing[0]
    sent_wave = waveform[order_list]
    sent_bins = length_bin[order_list]
    wave, bins = (
        lax.all_to_all(sent_wave, "dp", split_axis=0, concat_axis=0, tiled=True),
        lax.all_to_all(sent_bins, "dp", split_axis=0, concat_axis=0, tiled=True),
    )
    count = wave.shape[0]
    record = wave.shape[1]
    frames_two = cotangent.shape[1]
    width = cotangent.shape[2]
    groups = count // GROUP
    xs = (
        wave.reshape(groups, GROUP, record),
        bins.reshape(groups, GROUP),
        cotangent.reshape(groups, GROUP, frames_two, width),
    )

    def step(small_sum, item):
        cols_two, dz_two_b, small = pass_group(
            item[0],
            item[1],
            item[2],
            conv_one,
            bias_one,
            gain_one,
            shift_one,
            conv_two,
            bias_two,
            gain_two,
            shift_two,
        )
        return (small_sum + small, (cols_two, dz_two_b))

    small_local, stacked = lax.scan(step, jnp.zeros((16, width), jnp.float32), xs)
    cols_all = stacked[0].reshape(count * frames_two, 3 * width)
    dz_all = stacked[1].reshape(count * frames_two, width)
    term = lax.dot_general(
        cols_all, dz_all, (((0,), (0,)), ((), ())), preferred_element_type=jnp.float32
    )
    whole = lax.psum(term, "blk")
    share = lax.psum_scatter(whole, "dp", scatter_dimension=0, tiled=True)
    small_total = lax.psum(small_local, ("dp", "blk"))
    return (share, small_total)


def solution(mesh):
    return jax.shard_map(
        per_device,
        mesh=mesh,
        in_specs=(
            P(("dp", "blk"), None),
            P(("dp", "blk")),
            P(("dp", "blk"), None),
            P(("dp", "blk"), None, None),
            P(),
            P(),
            P(),
            P(),
            P(),
            P(),
            P(),
            P(),
        ),
        out_specs=(P("dp", None), P()),
        check_vma=False,
    )
```

profile of v0, /device:TPU:0, one launch (start us, length us, event | category | flops | bytes accessed | tf_op | source)
XLA Modules:
  0.0 192.3 jit_solution(11816954975854196462)
XLA Ops:
  7.2 0.7 fusion.21
  7.9 1.3 gather_fusion.1
  9.2 0.7 copy.29
  9.9 7.4 %all-to-all-start.1 = ((s32[16,1,1]{2,1,0:T(1,128)}), s32[16,1,1]{2,1,0:T(1,128)S(1)}, u32[]{:S(2)}, u32[]{:S(2)}) async-start(s32[16,1,1]{2,1,0:T(1,128)} %copy.29), calls=%async_computation.1 | async-start | bytes 16384 | tf_op jit(solution)/shard_map/all_to_all | solution.py:119
  17.2 0.6 gather_fusion
  17.8 0.5 broadcast.360
  18.3 0.7 reduce.1
  19.0 0.7 reshape.260
  19.7 3.9 %all-to-all-done.1 = s32[16,1,1]{2,1,0:T(1,128)S(1)} async-done(((s32[16,1,1]{2,1,0:T(1,128)}), s32[16,1,1]{2,1,0:T(1,128)S(1)}, u32[]{:S(2)}, u32[]{:S(2)}) %all-to-all-start.1) | async-done | bytes 96 | tf_op jit(solution)/shard_map/all_to_all | solution.py:119
  23.6 3.5 %all-to-all-start = ((bf16[16,2,165]{2,1,0:T(2,128)(2,1)}), bf16[16,2,165]{2,1,0:T(2,128)(2,1)S(1)}, u32[]{:S(2)}, u32[]{:S(2)}) async-start(bf16[16,2,165]{2,1,0:T(2,128)(2,1)} %reshape.260), calls=%async_computation | async-start | bytes 32768 | tf_op jit(solution)/shard_map/all_to_all | solution.py:118
  27.5 0.7 reshape.230
  28.2 5.3 %all-to-all-done = bf16[16,2,165]{2,1,0:T(2,128)(2,1)S(1)} async-done(((bf16[16,2,165]{2,1,0:T(2,128)(2,1)}), bf16[16,2,165]{2,1,0:T(2,128)(2,1)S(1)}, u32[]{:S(2)}, u32[]{:S(2)}) %all-to-all-start) | async-done | bytes 10592 | tf_op jit(solution)/shard_map/all_to_all | solution.py:118
  33.6 0.6 copy.35
  34.2 41.1 %while.17 = (s32[]{:T(128)}, f32[16,512]{1,0:T(8,128)}, bf16[2,256,1536]{2,1,0:T(8,128)(2,1)}, bf16[2,256,512]{2,1,0:T(8,128)(2,1)}, bf16[2,8,330]{2,1,0:T(8,128...) while((s32[]{:T(128)}, f32[16,512]{1,0:T(8,128)}, ...), condition=%wide.region_15.16_spmd.clone, body=%wide.region_0.15_spmd.clone.sunk | while | flops 835685888 | bytes 56027588 | solution.py:148
  34.2 0.7 and_select_fusion.2
  35.1 0.7 constant_dynamic-slice_fusion.5
  36.6 0.4 fusion.58
  39.0 2.1 %fusion.59 = (f32[256]{0:T(256)S(1)}, f32[256,512]{1,0:T(8,128)S(1)}) fusion(f32[512]{0:T(512)S(1)} %copy-done.11, bf16[1536,512]{1,0:T(8,128)(2,1)} %get-tuple-element.475, bf16[256,512]{1,0:T(8,128)(2,1)S(1)} %bitcast.85, bf16[256,1024]{1,0:T(8,128)(2,1)S(1)} %concatenate.58), kind=kOutput, calls=%fused_computation.73.clone.1 | convolution fusion | flops 404487936 | bytes 2886656 | tf_op jit(solution)/shard_map/while/body/eval_jaxpr/dot_general | solution.py:64
  41.4 0.6 multiply_reduce_fusion.14
  42.4 0.8 copy-done.10
  43.3 0.9 maximum_dynamic-update-slice_fusion.2
  44.2 0.8 copy-done.1
  45.0 0.6 fusion.61
  45.6 0.8 slice_bitcast_fusion.2
  46.7 1.6 copy.42
  48.6 1.7 reshape.273
  50.4 1.5 pad_add_fusion.2
  52.0 1.1 multiply_reduce_fusion.15
  53.8 0.6 select_add_fusion.2
  54.4 0.7 and_select_fusion.2
  55.3 0.7 constant_dynamic-slice_fusion.5
  56.8 0.4 fusion.58
  59.2 2.1 %fusion.59 = (f32[256]{0:T(256)S(1)}, f32[256,512]{1,0:T(8,128)S(1)}) fusion(f32[512]{0:T(512)S(1)} %copy-done.11, bf16[1536,512]{1,0:T(8,128)(2,1)} %get-tuple-element.475, bf16[256,512]{1,0:T(8,128)(2,1)S(1)} %bitcast.85, bf16[256,1024]{1,0:T(8,128)(2,1)S(1)} %concatenate.58), kind=kOutput, calls=%fused_computation.73.clone.1 | convolution fusion | flops 404487936 | bytes 2886656 | tf_op jit(solution)/shard_map/while/body/eval_jaxpr/dot_general | solution.py:64
  61.6 0.6 multiply_reduce_fusion.14
  62.6 0.8 copy-done.10
  63.5 0.9 maximum_dynamic-update-slice_fusion.2
  64.4 0.8 copy-done.1
  65.2 0.6 fusion.61
  65.8 0.8 slice_bitcast_fusion.2
  66.9 1.6 copy.42
  68.8 1.7 reshape.273
  70.6 1.5 pad_add_fusion.2
  72.2 1.1 multiply_reduce_fusion.15
  74.0 1.4 select_add_fusion.2
  75.4 4.2 %convolution_bitcast_fusion = f32[1536,512]{1,0:T(8,128)} fusion(bf16[2,256,1536]{2,1,0:T(8,128)(2,1)} %get-tuple-element.190, bf16[2,256,512]{2,1,0:T(8,128)(2,1)} %get-tuple-element.191), kind=kOutput, calls=%fused_computation.65 | convolution fusion | flops 805306368 | bytes 5242880 | tf_op jit(solution)/shard_map/dot_general | solution.py:151
  79.6 63.6 %reduce-scatter.2.cloned.1.call-done = f32[96,512]{1,0:T(8,128)} async-done(((f32[1536,512]{1,0:T(8,128)}), f32[96,512]{1,0:T(8,128)}) %reduce-scatter.2.cloned.1.call-update) | async-done | bytes 196624 | tf_op jit(solution)/shard_map/reduce_scatter | solution.py:155
  143.3 40.6 %psum.15 = f32[16,512]{1,0:T(8,128)} all-reduce(f32[16,512]{1,0:T(8,128)} %get-tuple-element.192), channel_id=1, replica_groups=mesh['dp'=16,'blk'=2] {'dp','blk'}, use_global_device_ids=true, to_apply=%region_18.19 | all-reduce | flops 8192 | bytes 65536 | tf_op jit(solution)/shard_map/psum | solution.py:156
  183.9 1.6 copy.58
  (119 shorter events, 10.3 us)
Async XLA Ops:
  7.2 10.1 %copy-start = (bf16[16,330]{1,0:T(8,128)(2,1)S(1)}, bf16[16,330]{1,0:T(8,128)(2,1)}, u32[]{:S(2)}) copy-start(bf16[16,330]{1,0:T(8,128)(2,1)} %param.14) | copy-start | bytes 31684
  9.9 13.7 %all-to-all-start.1 = ((s32[16,1,1]{2,1,0:T(1,128)}), s32[16,1,1]{2,1,0:T(1,128)S(1)}, u32[]{:S(2)}, u32[]{:S(2)}) async-start(s32[16,1,1]{2,1,0:T(1,128)} %copy.29), calls=%async_computation.1 | async-start | bytes 16384 | tf_op jit(solution)/shard_map/all_to_all | solution.py:119
  23.6 10.0 %all-to-all-start = ((bf16[16,2,165]{2,1,0:T(2,128)(2,1)}), bf16[16,2,165]{2,1,0:T(2,128)(2,1)S(1)}, u32[]{:S(2)}, u32[]{:S(2)}) async-start(bf16[16,2,165]{2,1,0:T(2,128)(2,1)} %reshape.260), calls=%async_computation | async-start | bytes 32768 | tf_op jit(solution)/shard_map/all_to_all | solution.py:118
  27.1 116.2 %reduce-scatter.2.cloned.1.call-start = ((), (), s32[]{:S(2)}) async-start(), calls=%async_computation.3 | async-start | bytes 3342336 | tf_op jit(solution)/shard_map/reduce_scatter | solution.py:155
  34.2 2.3 %copy-start.2 = (bf16[2,8,32,512]{3,2,1,0:T(8,128)(2,1)S(1)}, bf16[2,8,32,512]{3,2,1,0:T(8,128)(2,1)}, u32[]{:S(2)}) copy-start(bf16[2,8,32,512]{3,2,1,0:T(8,128)(2,1)} %get-tuple-element.477) | copy-start | bytes 1572868 | tf_op jit(solution)/shard_map/while
  34.2 2.3 %copy-start.4 = (bf16[10,512]{1,0:T(8,128)(2,1)S(1)}, bf16[10,512]{1,0:T(8,128)(2,1)}, u32[]{:S(2)}) copy-start(bf16[10,512]{1,0:T(8,128)(2,1)} %get-tuple-element.471) | copy-start | bytes 30724 | tf_op jit(solution)/shard_map/while
  34.2 2.3 %copy-start.7 = (f32[512]{0:T(512)S(1)}, f32[512]{0:T(512)}, u32[]{:S(2)}) copy-start(f32[512]{0:T(512)} %get-tuple-element.472) | copy-start | bytes 6148 | tf_op jit(solution)/shard_map/while
  36.5 0.8 copy-start.3
  36.5 0.8 copy-start.5
  38.4 0.7 copy-start.11
  39.0 2.3 %copy-start.6 = (f32[512]{0:T(512)S(1)}, f32[512]{0:T(512)}, u32[]{:S(2)}) copy-start(f32[512]{0:T(512)} %get-tuple-element.479) | copy-start | bytes 6148 | tf_op jit(solution)/shard_map/while
  39.0 2.3 %copy-start.8 = (f32[512]{0:T(512)S(1)}, f32[512]{0:T(512)}, u32[]{:S(2)}) copy-start(f32[512]{0:T(512)} %get-tuple-element.480) | copy-start | bytes 6148 | tf_op jit(solution)/shard_map/while
  41.1 1.0 copy-start.9
  42.4 0.8 copy-start.10
  43.3 1.7 copy-start.1
  54.4 2.3 %copy-start.2 = (bf16[2,8,32,512]{3,2,1,0:T(8,128)(2,1)S(1)}, bf16[2,8,32,512]{3,2,1,0:T(8,128)(2,1)}, u32[]{:S(2)}) copy-start(bf16[2,8,32,512]{3,2,1,0:T(8,128)(2,1)} %get-tuple-element.477) | copy-start | bytes 1572868 | tf_op jit(solution)/shard_map/while
  54.4 2.3 %copy-start.4 = (bf16[10,512]{1,0:T(8,128)(2,1)S(1)}, bf16[10,512]{1,0:T(8,128)(2,1)}, u32[]{:S(2)}) copy-start(bf16[10,512]{1,0:T(8,128)(2,1)} %get-tuple-element.471) | copy-start | bytes 30724 | tf_op jit(solution)/shard_map/while
  54.4 2.3 %copy-start.7 = (f32[512]{0:T(512)S(1)}, f32[512]{0:T(512)}, u32[]{:S(2)}) copy-start(f32[512]{0:T(512)} %get-tuple-element.472) | copy-start | bytes 6148 | tf_op jit(solution)/shard_map/while
  56.7 0.8 copy-start.3
  56.7 0.8 copy-start.5
  58.6 0.7 copy-start.11
  59.2 2.3 %copy-start.6 = (f32[512]{0:T(512)S(1)}, f32[512]{0:T(512)}, u32[]{:S(2)}) copy-start(f32[512]{0:T(512)} %get-tuple-element.479) | copy-start | bytes 6148 | tf_op jit(solution)/shard_map/while
  59.2 2.3 %copy-start.8 = (f32[512]{0:T(512)S(1)}, f32[512]{0:T(512)}, u32[]{:S(2)}) copy-start(f32[512]{0:T(512)} %get-tuple-element.480) | copy-start | bytes 6148 | tf_op jit(solution)/shard_map/while
  61.3 1.0 copy-start.9
  62.6 0.8 copy-start.10
  63.5 1.7 copy-start.1
  79.6 104.3 %all-reduce.5.cloned.1.call-start = ((), (), s32[]{:S(2)}) async-start(), calls=%async_computation.4 | async-start | bytes 393216 | tf_op jit(solution)/shard_map/psum | solution.py:154
Sparse Core Ops, SparseCore 0:
  79.7 63.4 reduce-scatter.1
  145.5 21.4 all-reduce.4
where the time goes:
time: 193 us; the launch traced here: 192 us
  waiting for transfers between devices  72.8 us (38%)
  blocking collectives  40.6 us (21%)
  local copies, waits for them, and re-layouts  25.6 us (13%)
  other arithmetic  16.9 us (9%)
  between operations  14.1 us (7%)
  starting transfers between devices  10.9 us (6%)
  matrix products  10.8 us (6%)
    reduce_scatter x1, waiting for transfers between devices, per_device(): share = lax.psum_scatter(whole, 'dp', scatter_dimension=0, tiled=True)  63.6 us
    psum x1, blocking collectives, per_device(): small_total = lax.psum(small_local, ('dp', 'blk'))  40.6 us
    all_to_all x1, starting transfers between devices, per_device(): lax.all_to_all(sent_bins, 'dp', split_axis=0, concat_axis=0, tiled=True)  7.36 us
    while x46, local copies, waits for them, and re-layouts  7.26 us
    all_to_all x1, waiting for transfers between devices, per_device(): lax.all_to_all(sent_wave, 'dp', split_axis=0, concat_axis=0, tiled=True)  5.32 us
    dot_general x2, matrix products, pass_group(): jnp.dot(cols_two, conv_two, preferred_element_type=jnp.float32) + bias_two  4.2 us
    dot_general x1, matrix products, per_device(): lax.dot_general(cols_all, dz_all, (((0,), (0,)), ((), ())), preferred_ele...  4.2 us
    all_to_all x1, waiting for transfers between devices, per_device(): lax.all_to_all(sent_bins, 'dp', split_axis=0, concat_axis=0, tiled=True)  3.87 us
  transfers between devices with their start and end apart: 4, of which 3 were waited for; matrix products, arithmetic and copies ran while one was open for 2% of the time, Pallas kernels for 0%

commit v1 on v0

--- a/solution.py
+++ b/solution.py
@@ -153,7 +153,7 @@
     )
     whole = lax.psum(term, "blk")
     share = lax.psum_scatter(whole, "dp", scatter_dimension=0, tiled=True)
-    small_total = lax.psum(small_local, ("dp", "blk"))
+    small_total = lax.all_gather(small_local, ("dp", "blk")).sum(axis=0)
     return (share, small_total)
 
 

time: 193 us -> 178 us (0.922)
  blocking collectives: 40.6 us -> 0 us
  waiting for transfers between devices: 72.8 us -> 94.9 us
    psum x1 -> x0, blocking collectives: 40.6 us -> none  [per_device(): small_total = lax.psum(small_local, ('dp', 'blk'))]
    psum x1, waiting for transfers between devices: 0.01 us -> 19.9 us  [per_device(): whole = lax.psum(term, 'blk')]
  transfers between devices with their start and end apart: 4 -> 5, of which waited for: 3 -> 5; matrix products, arithmetic and copies ran while one was open for 2% -> 3% of each run, Pallas kernels for 0% -> 0%
where the time goes in v1:
time: 178 us; the launch traced here: 177 us
  waiting for transfers between devices  94.9 us (53%)
  local copies, waits for them, and re-layouts  25.6 us (14%)
  other arithmetic  18.8 us (11%)
  between operations  15.6 us (9%)
  starting transfers between devices  11 us (6%)
  matrix products  10.8 us (6%)
    reduce_scatter x1, waiting for transfers between devices, per_device(): share = lax.psum_scatter(whole, 'dp', scatter_dimension=0, tiled=True)  63.6 us
    psum x1, waiting for transfers between devices, per_device(): whole = lax.psum(term, 'blk')  19.9 us
    all_to_all x1, starting transfers between devices, per_device(): lax.all_to_all(sent_bins, 'dp', split_axis=0, concat_axis=0, tiled=True)  7.36 us
    while x46, local copies, waits for them, and re-layouts  7.26 us
    all_to_all x1, waiting for transfers between devices, per_device(): lax.all_to_all(sent_wave, 'dp', split_axis=0, concat_axis=0, tiled=True)  5.32 us
    dot_general x2, matrix products, pass_group(): jnp.dot(cols_two, conv_two, preferred_element_type=jnp.float32) + bias_two  4.2 us
    dot_general x1, matrix products, per_device(): lax.dot_general(cols_all, dz_all, (((0,), (0,)), ((), ())), preferred_ele...  4.2 us
    all_to_all x1, waiting for transfers between devices, per_device(): lax.all_to_all(sent_bins, 'dp', split_axis=0, concat_axis=0, tiled=True)  3.87 us
  transfers between devices with their start and end apart: 5, of which 5 were waited for; matrix products, arithmetic and copies ran while one was open for 3% of the time, Pallas kernels for 0%

profile of v1, /device:TPU:0, one launch (start us, length us, event | category | flops | bytes accessed | tf_op | source)
XLA Modules:
  0.0 177.2 jit_solution(14869388647237857085)
XLA Ops:
  8.0 0.7 fusion.21
  8.7 1.3 gather_fusion.1
  10.0 0.7 copy.29
  10.7 7.4 %all-to-all-start.1 = ((s32[16,1,1]{2,1,0:T(1,128)}), s32[16,1,1]{2,1,0:T(1,128)S(1)}, u32[]{:S(2)}, u32[]{:S(2)}) async-start(s32[16,1,1]{2,1,0:T(1,128)} %copy.29), calls=%async_computation.1 | async-start | bytes 16384 | tf_op jit(solution)/shard_map/all_to_all | solution.py:119
  18.1 0.6 gather_fusion
  19.2 0.7 reduce.1
  19.8 0.7 reshape.261
  20.5 3.9 %all-to-all-done.1 = s32[16,1,1]{2,1,0:T(1,128)S(1)} async-done(((s32[16,1,1]{2,1,0:T(1,128)}), s32[16,1,1]{2,1,0:T(1,128)S(1)}, u32[]{:S(2)}, u32[]{:S(2)}) %all-to-all-start.1) | async-done | bytes 96 | tf_op jit(solution)/shard_map/all_to_all | solution.py:119
  24.4 3.5 %all-to-all-start = ((bf16[16,2,165]{2,1,0:T(2,128)(2,1)}), bf16[16,2,165]{2,1,0:T(2,128)(2,1)S(1)}, u32[]{:S(2)}, u32[]{:S(2)}) async-start(bf16[16,2,165]{2,1,0:T(2,128)(2,1)} %reshape.261), calls=%async_computation | async-start | bytes 32768 | tf_op jit(solution)/shard_map/all_to_all | solution.py:118
  28.3 0.7 reshape.230
  29.0 5.3 %all-to-all-done = bf16[16,2,165]{2,1,0:T(2,128)(2,1)S(1)} async-done(((bf16[16,2,165]{2,1,0:T(2,128)(2,1)}), bf16[16,2,165]{2,1,0:T(2,128)(2,1)S(1)}, u32[]{:S(2)}, u32[]{:S(2)}) %all-to-all-start) | async-done | bytes 10592 | tf_op jit(solution)/shard_map/all_to_all | solution.py:118
  34.4 0.6 copy.35
  35.0 41.1 %while.17 = (s32[]{:T(128)}, f32[16,512]{1,0:T(8,128)}, bf16[2,256,1536]{2,1,0:T(8,128)(2,1)}, bf16[2,256,512]{2,1,0:T(8,128)(2,1)}, bf16[2,8,330]{2,1,0:T(8,128...) while((s32[]{:T(128)}, f32[16,512]{1,0:T(8,128)}, ...), condition=%wide.region_15.16_spmd.clone, body=%wide.region_0.15_spmd.clone.sunk | while | flops 835685888 | bytes 56027588 | solution.py:148
  35.1 0.7 and_select_fusion.2
  36.0 0.7 constant_dynamic-slice_fusion.5
  39.9 2.1 %fusion.59 = (f32[256]{0:T(256)S(1)}, f32[256,512]{1,0:T(8,128)S(1)}) fusion(f32[512]{0:T(512)S(1)} %copy-done.11, bf16[1536,512]{1,0:T(8,128)(2,1)} %get-tuple-element.475, bf16[256,512]{1,0:T(8,128)(2,1)S(1)} %bitcast.86, bf16[256,1024]{1,0:T(8,128)(2,1)S(1)} %concatenate.58), kind=kOutput, calls=%fused_computation.73.clone.1 | convolution fusion | flops 404487936 | bytes 2886656 | tf_op jit(solution)/shard_map/while/body/eval_jaxpr/dot_general | solution.py:64
  42.2 0.6 multiply_reduce_fusion.14
  43.3 0.8 copy-done.10
  44.1 0.9 maximum_dynamic-update-slice_fusion.2
  45.1 0.8 copy-done.1
  45.8 0.6 fusion.61
  46.4 0.8 slice_bitcast_fusion.2
  47.5 1.6 copy.42
  49.5 1.7 reshape.274
  51.2 1.5 pad_add_fusion.2
  52.9 1.1 multiply_reduce_fusion.15
  54.6 0.6 select_add_fusion.2
  55.3 0.7 and_select_fusion.2
  56.2 0.7 constant_dynamic-slice_fusion.5
  60.1 2.1 %fusion.59 = (f32[256]{0:T(256)S(1)}, f32[256,512]{1,0:T(8,128)S(1)}) fusion(f32[512]{0:T(512)S(1)} %copy-done.11, bf16[1536,512]{1,0:T(8,128)(2,1)} %get-tuple-element.475, bf16[256,512]{1,0:T(8,128)(2,1)S(1)} %bitcast.86, bf16[256,1024]{1,0:T(8,128)(2,1)S(1)} %concatenate.58), kind=kOutput, calls=%fused_computation.73.clone.1 | convolution fusion | flops 404487936 | bytes 2886656 | tf_op jit(solution)/shard_map/while/body/eval_jaxpr/dot_general | solution.py:64
  62.4 0.6 multiply_reduce_fusion.14
  63.5 0.8 copy-done.10
  64.3 0.9 maximum_dynamic-update-slice_fusion.2
  65.3 0.8 copy-done.1
  66.0 0.6 fusion.61
  66.6 0.8 slice_bitcast_fusion.2
  67.7 1.6 copy.42
  69.7 1.7 reshape.274
  71.4 1.5 pad_add_fusion.2
  73.1 1.1 multiply_reduce_fusion.15
  74.8 1.4 select_add_fusion.2
  76.2 4.2 %convolution_bitcast_fusion = f32[1536,512]{1,0:T(8,128)} fusion(bf16[2,256,1536]{2,1,0:T(8,128)(2,1)} %get-tuple-element.190, bf16[2,256,512]{2,1,0:T(8,128)(2,1)} %get-tuple-element.191), kind=kOutput, calls=%fused_computation.65 | convolution fusion | flops 805306368 | bytes 5242880 | tf_op jit(solution)/shard_map/dot_general | solution.py:151
  80.5 0.5 all-gather.3.cloned.1.call-update
  81.0 63.6 %reduce-scatter.2.cloned.1.call-done = f32[96,512]{1,0:T(8,128)} async-done(((f32[1536,512]{1,0:T(8,128)}), f32[96,512]{1,0:T(8,128)}) %reduce-scatter.2.cloned.1.call-update) | async-done | bytes 196624 | tf_op jit(solution)/shard_map/reduce_scatter | solution.py:155
  144.7 1.6 all-gather.3.cloned.1.call-done
  146.3 1.9 %reduce_sum.177 = f32[16,512]{1,0:T(8,128)} reduce(f32[32,16,512]{2,1,0:T(8,128)} %bitcast.89, f32[]{:T(128)} %constant.127.clone.1), dimensions={0}, to_apply=%region_18.19 | reduce | flops 253952 | bytes 1081348 | tf_op jit(solution)/shard_map/reduce_sum | solution.py:156
  148.3 19.9 %all-reduce.5.cloned.1.call-done = f32[96,512]{1,0:T(8,128)} async-done(((f32[96,512]{1,0:T(8,128)}), f32[96,512]{1,0:T(8,128)}) %all-reduce.5.cloned.1.call-update) | async-done | bytes 196624 | tf_op jit(solution)/shard_map/psum | solution.py:154
  168.2 1.6 copy.58
  (122 shorter events, 11.7 us)
Async XLA Ops:
  8.0 10.1 %copy-start = (bf16[16,330]{1,0:T(8,128)(2,1)S(1)}, bf16[16,330]{1,0:T(8,128)(2,1)}, u32[]{:S(2)}) copy-start(bf16[16,330]{1,0:T(8,128)(2,1)} %param.14) | copy-start | bytes 31684
  10.7 13.7 %all-to-all-start.1 = ((s32[16,1,1]{2,1,0:T(1,128)}), s32[16,1,1]{2,1,0:T(1,128)S(1)}, u32[]{:S(2)}, u32[]{:S(2)}) async-start(s32[16,1,1]{2,1,0:T(1,128)} %copy.29), calls=%async_computation.1 | async-start | bytes 16384 | tf_op jit(solution)/shard_map/all_to_all | solution.py:119
  24.4 10.0 %all-to-all-start = ((bf16[16,2,165]{2,1,0:T(2,128)(2,1)}), bf16[16,2,165]{2,1,0:T(2,128)(2,1)S(1)}, u32[]{:S(2)}, u32[]{:S(2)}) async-start(bf16[16,2,165]{2,1,0:T(2,128)(2,1)} %reshape.261), calls=%async_computation | async-start | bytes 32768 | tf_op jit(solution)/shard_map/all_to_all | solution.py:118
  27.9 116.8 %reduce-scatter.2.cloned.1.call-start = ((), (), s32[]{:S(2)}) async-start(), calls=%async_computation.4 | async-start | bytes 3342336 | tf_op jit(solution)/shard_map/reduce_scatter | solution.py:155
  35.0 2.3 %copy-start.2 = (bf16[2,8,32,512]{3,2,1,0:T(8,128)(2,1)S(1)}, bf16[2,8,32,512]{3,2,1,0:T(8,128)(2,1)}, u32[]{:S(2)}) copy-start(bf16[2,8,32,512]{3,2,1,0:T(8,128)(2,1)} %get-tuple-element.477) | copy-start | bytes 1572868 | tf_op jit(solution)/shard_map/while
  35.1 2.3 %copy-start.4 = (bf16[10,512]{1,0:T(8,128)(2,1)S(1)}, bf16[10,512]{1,0:T(8,128)(2,1)}, u32[]{:S(2)}) copy-start(bf16[10,512]{1,0:T(8,128)(2,1)} %get-tuple-element.471) | copy-start | bytes 30724 | tf_op jit(solution)/shard_map/while
  35.1 2.3 %copy-start.7 = (f32[512]{0:T(512)S(1)}, f32[512]{0:T(512)}, u32[]{:S(2)}) copy-start(f32[512]{0:T(512)} %get-tuple-element.472) | copy-start | bytes 6148 | tf_op jit(solution)/shard_map/while
  37.4 0.8 copy-start.3
  37.4 0.8 copy-start.5
  39.2 0.7 copy-start.11
  39.9 2.3 %copy-start.6 = (f32[512]{0:T(512)S(1)}, f32[512]{0:T(512)}, u32[]{:S(2)}) copy-start(f32[512]{0:T(512)} %get-tuple-element.479) | copy-start | bytes 6148 | tf_op jit(solution)/shard_map/while
  39.9 2.3 %copy-start.8 = (f32[512]{0:T(512)S(1)}, f32[512]{0:T(512)}, u32[]{:S(2)}) copy-start(f32[512]{0:T(512)} %get-tuple-element.480) | copy-start | bytes 6148 | tf_op jit(solution)/shard_map/while
  42.0 1.0 copy-start.9
  43.3 0.8 copy-start.10
  44.1 1.7 copy-start.1
  55.2 2.3 %copy-start.2 = (bf16[2,8,32,512]{3,2,1,0:T(8,128)(2,1)S(1)}, bf16[2,8,32,512]{3,2,1,0:T(8,128)(2,1)}, u32[]{:S(2)}) copy-start(bf16[2,8,32,512]{3,2,1,0:T(8,128)(2,1)} %get-tuple-element.477) | copy-start | bytes 1572868 | tf_op jit(solution)/shard_map/while
  55.2 2.3 %copy-start.4 = (bf16[10,512]{1,0:T(8,128)(2,1)S(1)}, bf16[10,512]{1,0:T(8,128)(2,1)}, u32[]{:S(2)}) copy-start(bf16[10,512]{1,0:T(8,128)(2,1)} %get-tuple-element.471) | copy-start | bytes 30724 | tf_op jit(solution)/shard_map/while
  55.3 2.3 %copy-start.7 = (f32[512]{0:T(512)S(1)}, f32[512]{0:T(512)}, u32[]{:S(2)}) copy-start(f32[512]{0:T(512)} %get-tuple-element.472) | copy-start | bytes 6148 | tf_op jit(solution)/shard_map/while
  57.6 0.8 copy-start.3
  57.6 0.8 copy-start.5
  59.4 0.7 copy-start.11
  60.1 2.3 %copy-start.6 = (f32[512]{0:T(512)S(1)}, f32[512]{0:T(512)}, u32[]{:S(2)}) copy-start(f32[512]{0:T(512)} %get-tuple-element.479) | copy-start | bytes 6148 | tf_op jit(solution)/shard_map/while
  60.1 2.3 %copy-start.8 = (f32[512]{0:T(512)S(1)}, f32[512]{0:T(512)}, u32[]{:S(2)}) copy-start(f32[512]{0:T(512)} %get-tuple-element.480) | copy-start | bytes 6148 | tf_op jit(solution)/shard_map/while
  62.2 1.0 copy-start.9
  63.4 0.8 copy-start.10
  64.3 1.7 copy-start.1
  80.4 65.9 %all-gather.3.cloned.1.call-start = ((), (), s32[]{:S(2)}) async-start(), calls=%async_computation.3 | async-start | bytes 1081344 | tf_op jit(solution)/shard_map/all_gather | solution.py:156
  81.0 87.2 %all-reduce.5.cloned.1.call-start = ((), (), s32[]{:S(2)}) async-start(), calls=%async_computation.5 | async-start | bytes 393216 | tf_op jit(solution)/shard_map/psum | solution.py:154
Sparse Core Ops, SparseCore 0:
  80.5 64.1 reduce-scatter.1
  147.0 21.1 all-reduce.4
Sparse Core Ops, SparseCore 1:
  84.4 61.8 all-gather.2
